TPU v7x, 32 devices: a whole 2x2x4 slice. The times are simulated.
32 devices in a mesh: parts: 2 (over x), node: 2 (over core), lane: 8 (over z, y).
Axes of the slice: x: 2, y: 2, z: 4, core: 2. Of those that a mesh axis runs over, the one named last changes fastest.
Arguments:
- quant_rows: bfloat16 [1024, 7168], P(('parts', 'node', 'lane')), parts along dimension 0, may hold values from -6 to 6
- block_scales: bfloat16 [1024, 56], P(('parts', 'node', 'lane')), parts along dimension 0, may hold values from 0.5 to 2
- expert_ids: int32 [1024, 4], P(('parts', 'node', 'lane')), parts along dimension 0, may hold values from 0 to 7, all different within a row; in each aligned block of 32 rows (0 to 31, 32 to 63, ...) at most 24 rows name the same one
- route_gates: bfloat16 [1024, 4], P(('parts', 'node', 'lane')), parts along dimension 0, may hold values from 0.19921875 to 1
- gate_proj: bfloat16 [16, 7168, 1024], P(('node', 'lane')), may hold values from -0.0625 to 0.0625
- up_proj: bfloat16 [16, 7168, 1024], P(('node', 'lane')), may hold values from -0.0625 to 0.0625
- down_proj: bfloat16 [16, 1024, 7168], P(('node', 'lane')), may hold values from -0.125 to 0.125
Outputs:
- moe_output: bfloat16 [1024, 7168], P(('parts', 'node', 'lane')), parts along dimension 0
There are 2 independent parts, one for each index of `parts`. A program takes and returns all parts, laid end to end along the dimension named above; an argument that names none is the same for every part. Nothing has to cross between parts.
Inputs may be any that keep to these rules, and one draw needn't show every extreme that they name: `expert_ids`: each row names 4 different experts. Among the 32 rows of one device no expert is named by more than 24 rows, and in every draw some device has an expert named by exactly 24 of its rows.
All inputs are finite; a program needn't handle non-finite values.
Results may differ from a plain program's by a relative error of at most 0.012.
Values may be sent and summed in bfloat16 or wider, within the bound.
A program may use at most 192 MiB of HBM per device.

v0:
```python
from functools import partial

import jax
import jax.numpy as jnp
from jax import lax
from jax.sharding import PartitionSpec as P

EXP_GRP = 4


def dequantize(quant_part, scale_part):
    row_total, feature_total = quant_part.shape
    block_total = scale_part.shape[1]
    scaled = (
        quant_part.astype(jnp.float32).reshape(row_total, block_total, feature_total // block_total)
        * scale_part.astype(jnp.float32)[:, :, None]
    )
    return scaled.reshape(row_total, feature_total).astype(jnp.bfloat16)


def expert_terms(quant_part, scale_part, gate_column, gate_proj, up_proj, down_proj):
    inputs = dequantize(quant_part, scale_part)
    gate_out = jnp.dot(inputs, gate_proj[0], preferred_element_type=jnp.float32)
    up_out = jnp.dot(inputs, up_proj[0], preferred_element_type=jnp.float32)
    hidden = (jax.nn.silu(gate_out) * up_out).astype(jnp.bfloat16)
    projected = jnp.dot(hidden, down_proj[0], preferred_element_type=jnp.float32)
    return gate_column.astype(jnp.float32)[:, None] * projected


def local(quant_rows, block_scales, expert_ids, route_gates, gate_proj, up_proj, down_proj):
    node_total = lax.axis_size("node")
    lane_total = lax.axis_size("lane")
    span_count = lane_total // EXP_GRP
    expert_total = EXP_GRP * node_total
    expert_work = partial(expert_terms, gate_proj=gate_proj, up_proj=up_proj, down_proj=down_proj)
    labels = jnp.arange(expert_total, dtype=jnp.int32)
    weights = jnp.sum(
        jnp.where(
            expert_ids[:, :, None] == labels[None, None, :],
            route_gates.astype(jnp.float32)[:, :, None],
            0.0,
        ),
        axis=1,
    ).astype(jnp.bfloat16)
    all_quant, all_scales, all_weights = (
        lax.all_gather(quant_rows, ("node", "lane"), axis=0, tiled=True),
        lax.all_gather(block_scales, ("node", "lane"), axis=0, tiled=True),
        lax.all_gather(weights, ("node", "lane"), axis=0, tiled=True),
    )
    own_expert = lax.axis_index("node") * EXP_GRP + lax.axis_index("lane") // span_count
    column = lax.dynamic_index_in_dim(all_weights, own_expert, 1, keepdims=False)
    summed = lax.psum_scatter(
        expert_work(all_quant, all_scales, column).astype(jnp.bfloat16),
        ("node", "lane"),
        scatter_dimension=0,
        tiled=True,
    )
    return summed


def solution(mesh):
    placed = (
        P(("parts", "node", "lane"), None),
        P(("parts", "node", "lane"), None),
        P(("parts", "node", "lane"), None),
        P(("parts", "node", "lane"), None),
        P(("node", "lane"), None, None),
        P(("node", "lane"), None, None),
        P(("node", "lane"), None, None),
    )
    return jax.shard_map(
        local,
        mesh=mesh,
        in_specs=placed,
        out_specs=P(("parts", "node", "lane"), None),
        check_vma=False,
    )
```

profile of v0, /device:TPU:16, one launch (start us, length us, event | category | flops | bytes accessed | tf_op | source)
XLA Modules:
  0.0 238.4 jit_solution(18103597800439800031)
XLA Ops:
  6.5 0.0 all-gather.3.cloned.1.call-start
  6.5 0.7 all-gather.3.cloned.1.call-update
  7.3 0.0 reduce-scatter.2.cloned.1.call-start
  7.3 0.7 convert_element_type.23
  8.0 0.7 select_reduce_fusion
  8.7 29.0 %all-gather = bf16[16,32,8]{1,2,0:T(8,128)(2,1)S(1)} all-gather(bf16[1,32,8]{1,2,0:T(8,128)(2,1)S(1)} %bitcast.29), channel_id=1, replica_groups=mesh['parts'=2,'node'=2,'lane'=8] {'node','lane'}, dimensions={0}, use_global_device_ids=true | all-gather | bytes 8704 | tf_op jit(solution)/shard_map/all_gather | solution.py:48
  37.7 0.1 reshape.8
  37.8 31.1 %all_gather.11 = bf16[512,56]{1,0:T(8,128)(2,1)S(1)} all-gather(bf16[32,56]{1,0:T(8,128)(2,1)} %param.8), channel_id=1, replica_groups=mesh['parts'=2,'node'=2,'lane'=8] {'node','lane'}, dimensions={0}, use_global_device_ids=true | all-gather | bytes 60928 | tf_op jit(solution)/shard_map/all_gather | solution.py:47
  68.9 11.5 %all-gather.3.cloned.1.call-done = bf16[512,7168]{1,0:T(8,128)(2,1)} async-done(((bf16[32,7168]{1,0:T(8,128)(2,1)}), bf16[512,7168]{1,0:T(8,128)(2,1)}) %all-gather.3.cloned.1.call-update) | async-done | bytes 7340048 | tf_op jit(solution)/shard_map/all_gather | solution.py:46
  80.3 8.9 %mul.38 = f32[512,56,128]{2,1,0:T(8,128)} broadcast(bf16[512,56]{1,0:T(8,128)(2,1)S(1)} %all_gather.11), dimensions={0,1} | broadcast | bytes 14737408 | tf_op jit(solution)/shard_map/mul | solution.py:15
  89.2 18.4 %fusion.3 = f32[512,1024]{1,0:T(8,128)S(1)} fusion(bf16[1,7168,1024]{2,1,0:T(8,128)(2,1)} %param.12, f32[64,8,56,128]{3,2,1,0:T(8,128)} %bitcast.27, bf16[512,7168]{1,0:T(8,128)(2,1)} %all-gather.3.cloned.1.call-done), kind=kOutput, calls=%fused_computation.4 | convolution fusion | flops 7527202816 | bytes 38797312 | tf_op jit(solution)/shard_map/dot_general | solution.py:24
  107.6 17.7 %multiply_convert_fusion.1 = bf16[512,1024]{1,0:T(8,128)(2,1)S(1)} fusion(f32[512,1024]{1,0:T(8,128)S(1)} %fusion.3, bf16[1,7168,1024]{2,1,0:T(8,128)(2,1)} %param.11, f32[64,8,56,128]{3,2,1,0:T(8,128)} %bitcast.28, bf16[512,7168]{1,0:T(8,128)(2,1)} %all-gather.3.cloned.1.call-done), kind=kOutput, calls=%fused_computation.9 | convolution fusion | flops 7530348544 | bytes 39845888 | tf_op jit(solution)/shard_map/dot_general | solution.py:23
  125.3 15.2 %multiply_convert_fusion = bf16[512,7168]{1,0:T(8,128)(2,1)} fusion(bf16[512,1024]{1,0:T(8,128)(2,1)S(1)} %multiply_convert_fusion.1, bf16[1,1024,7168]{2,1,0:T(8,128)(2,1)} %param.13, f32[512]{0:T(512)S(1)} %bitcast.30), kind=kOutput, calls=%fused_computation.8 | convolution fusion | flops 7523532800 | bytes 23070720 | tf_op jit(solution)/shard_map/dot_general | solution.py:26
  140.5 0.0 reduce-scatter.2.cloned.1.call-update
  140.5 91.0 %reduce-scatter.2.cloned.1.call-done = bf16[32,7168]{1,0:T(8,128)(2,1)} async-done(((bf16[512,7168]{1,0:T(8,128)(2,1)}), bf16[32,7168]{1,0:T(8,128)(2,1)}) %reduce-scatter.2.cloned.1.call-update) | async-done | bytes 458768 | tf_op jit(solution)/shard_map/reduce_scatter | solution.py:52
  (2 shorter events, 0.0 us)
Async XLA Ops:
  6.5 73.8 %all-gather.3.cloned.1.call-start = ((), (), s32[]{:S(2)}) async-start(), calls=%async_computation.1 | async-start | bytes 7798784 | tf_op jit(solution)/shard_map/all_gather | solution.py:46
  7.3 224.3 %reduce-scatter.2.cloned.1.call-start = ((), (), s32[]{:S(2)}) async-start(), calls=%async_computation.2 | async-start | bytes 7798784 | tf_op jit(solution)/shard_map/reduce_scatter | solution.py:52
Sparse Core Ops, SparseCore 0:
  9.6 70.7 all-gather.2
  140.6 90.8 reduce-scatter.1
where the time goes:
time: 241 us; the launch traced here: 238 us
  waiting for transfers between devices  103 us (43%)
  blocking collectives  60.1 us (25%)
  matrix products  51.3 us (21%)
  between operations  13.4 us (6%)
  local copies, waits for them, and re-layouts  8.99 us (4%)
    reduce_scatter x1, waiting for transfers between devices, local(): lax.psum_scatter(expert_work(all_quant, all_scales, column).astype(jnp.bf...  91 us
    all_gather x1, blocking collectives, local(): lax.all_gather(block_scales, ('node', 'lane'), axis=0, tiled=True)  31.1 us
    all_gather x1, blocking collectives, local(): lax.all_gather(weights, ('node', 'lane'), axis=0, tiled=True)  29 us
    dot_general x1, matrix products, expert_terms(): up_out = jnp.dot(inputs, up_proj[0], preferred_element_type=jnp.float32)  18.4 us
    dot_general x1, matrix products, expert_terms(): gate_out = jnp.dot(inputs, gate_proj[0], preferred_element_type=jnp.float32)  17.7 us
    dot_general x1, matrix products, expert_terms(): jnp.dot(hidden, down_proj[0], preferred_element_type=jnp.float32)  15.2 us
    all_gather x1, waiting for transfers between devices, local(): lax.all_gather(quant_rows, ('node', 'lane'), axis=0, tiled=True)  11.5 us
    mul x1, local copies, waits for them, and re-layouts, dequantize(): quant_part.astype(jnp.float32)  8.88 us
  transfers between devices with their start and end apart: 2, of which 2 were waited for; matrix products, arithmetic and copies ran while one was open for 1% of the time, Pallas kernels for 0%

commit v1 on v0

v1 whole, which is shorter than its diff:
```python
import functools

import jax
import jax.numpy as jnp
from jax import lax
from jax.experimental import pallas as pl
from jax.experimental.pallas import tpu as pltpu
from jax.sharding import PartitionSpec as P

EXP_GRP = 4
Y = 2
CORES = 2
LANES = 128
TILE = 256
MESH = pl.DeviceIdType.MESH
F32 = jnp.float32
BF16 = jnp.bfloat16


def flip(value, bit):
    return value + bit - 2 * bit * ((value // bit) % 2)


def flip_all(value, mask):
    bit = 1
    while bit <= mask:
        if mask & bit:
            value = flip(value, bit)
        bit *= 2
    return value


def kernel(
    planes, pieces, span_count,
    quant_ref, scale_ref, ids_ref, gates_ref, gate_hbm, up_hbm, down_hbm,
    out_ref,
    gate_w, up_w, down_w, rows_buf, hidden, from_core, from_y, from_z,
    gate_sem, up_sem, down_sem,
    gz_send, gz_recv, gy_send, gy_recv, gc_send, gc_recv,
    rc_send, rc_recv, ry_send, ry_recv, rz_send, rz_recv,
):
    own, width = quant_ref.shape
    units = gate_w.shape[1]
    tiles = units // TILE
    group = CORES * Y * own
    part = width // pieces
    node, lane = lax.axis_index("node"), lax.axis_index("lane")
    z, y = lane // Y, lane % Y
    expert = node * EXP_GRP + lane // span_count

    def lane_z(mask):
        return {"lane": flip_all(z, mask) * Y + y}

    lane_y = {"lane": z * Y + (1 - y)}
    other_core = {"node": 1 - node}

    def weight_copies(j):
        cols = pl.ds(j * TILE, TILE)
        return (
            pltpu.make_async_copy(gate_hbm.at[0, :, cols], gate_w.at[:, cols], gate_sem.at[j]),
            pltpu.make_async_copy(up_hbm.at[0, :, cols], up_w.at[:, cols], up_sem.at[j]),
        )

    def down_copy(j):
        cols = pl.ds(j * part, part)
        return pltpu.make_async_copy(down_hbm.at[0, :, cols], down_w.at[:, cols], down_sem.at[j])

    for j in range(tiles):
        for copy in weight_copies(j):
            copy.start()
    for j in range(pieces):
        down_copy(j).start()

    barrier = pltpu.get_barrier_semaphore()
    for mask in range(1, planes):
        pl.semaphore_signal(barrier, inc=1, device_id=lane_z(mask), device_id_type=MESH)
    pl.semaphore_signal(barrier, inc=1, device_id=lane_y, device_id_type=MESH)
    pl.semaphore_signal(barrier, inc=1, device_id=other_core, device_id_type=MESH)

    labels = lax.broadcasted_iota(jnp.int32, (own, LANES), 1)
    route = jnp.zeros((own, LANES), F32)
    for k in range(ids_ref.shape[1]):
        route += jnp.where(
            ids_ref[:, k:k + 1] == labels, gates_ref[:, k:k + 1].astype(F32), 0.0
        )
    rows_buf[0:own, width:width + LANES] = route.astype(BF16)
    block = width // scale_ref.shape[1]
    for j in range(scale_ref.shape[1]):
        cols = slice(j * block, (j + 1) * block)
        rows_buf[0:own, cols] = (
            quant_ref[:, cols].astype(F32) * scale_ref[:, j:j + 1].astype(F32)
        ).astype(BF16)

    pl.semaphore_wait(barrier, planes - 1 + 2)

    def slot(g, c, v):
        return pl.ds(g * group + (c * Y + v) * own, own)

    def gz(g):
        bit = g & -g
        return pltpu.make_async_remote_copy(
            src_ref=rows_buf.at[slot(g ^ bit, 0, 0)], dst_ref=rows_buf.at[slot(g, 0, 0)],
            send_sem=gz_send.at[g], recv_sem=gz_recv.at[g],
            device_id=lane_z(bit), device_id_type=MESH)

    def gy(g):
        return pltpu.make_async_remote_copy(
            src_ref=rows_buf.at[slot(g, 0, 0)], dst_ref=rows_buf.at[slot(g, 0, 1)],
            send_sem=gy_send.at[g], recv_sem=gy_recv.at[g],
            device_id=lane_y, device_id_type=MESH)

    def gc(g, v):
        return pltpu.make_async_remote_copy(
            src_ref=rows_buf.at[slot(g, 0, v)], dst_ref=rows_buf.at[slot(g, 1, v)],
            send_sem=gc_send.at[g * Y + v], recv_sem=gc_recv.at[g * Y + v],
            device_id=other_core, device_id_type=MESH)

    def children(g):
        low = g & -g if g else planes
        bit, found = 1, []
        while bit < low and g + bit < planes:
            found.append(g + bit)
            bit *= 2
        return found

    def spread(g):
        if g:
            gz(g).wait_recv()
        for child in children(g):
            gz(child).start()
        gy(g).start()
        gc(g, 0).start()

    def pass_on(g):
        gy(g).wait_recv()
        gc(g, 1).start()

    def sends_done(g):
        for child in children(g):
            gz(child).wait_send()
        gy(g).wait_send()
        for v in range(Y):
            gc(g, v).wait_send()

    def cols_of(p):
        return pl.ds(p * part, part)

    def rc(g, p):
        return pltpu.make_async_remote_copy(
            src_ref=rows_buf.at[pl.ds(g * group + Y * own, Y * own), cols_of(p)],
            dst_ref=from_core.at[pl.ds(g * Y * own, Y * own), cols_of(p)],
            send_sem=rc_send.at[g * pieces + p], recv_sem=rc_recv.at[g * pieces + p],
            device_id=other_core, device_id_type=MESH)

    def ry(g, p):
        return pltpu.make_async_remote_copy(
            src_ref=rows_buf.at[slot(g, 0, 1), cols_of(p)],
            dst_ref=from_y.at[pl.ds(g * own, own), cols_of(p)],
            send_sem=ry_send.at[g * pieces + p], recv_sem=ry_recv.at[g * pieces + p],
            device_id=lane_y, device_id_type=MESH)

    def rz(g, p):
        return pltpu.make_async_remote_copy(
            src_ref=rows_buf.at[slot(g, 0, 0), cols_of(p)],
            dst_ref=from_z.at[pl.ds((g - 1) * own, own), cols_of(p)],
            send_sem=rz_send.at[(g - 1) * pieces + p], recv_sem=rz_recv.at[(g - 1) * pieces + p],
            device_id=lane_z(g), device_id_type=MESH)

    def add(rows, more, more_rows, p):
        @pl.loop(0, part // TILE)
        def _(i):
            cols = pl.ds(pl.multiple_of(p * part + i * TILE, TILE), TILE)
            rows_buf[rows, cols] = (
                rows_buf[rows, cols].astype(F32) + more[more_rows, cols].astype(F32)
            ).astype(BF16)

    def core_sum(g, p):
        rc(g, p).wait_recv()
        add(slot(g, 0, 1), from_core, pl.ds((g * Y + 1) * own, own), p)
        ry(g, p).start()
        add(slot(g, 0, 0), from_core, pl.ds(g * Y * own, own), p)

    def y_sum(g, p):
        ry(g, p).wait_recv()
        add(slot(g, 0, 0), from_y, pl.ds(g * own, own), p)
        if g:
            rz(g, p).start()

    def gate_up(g):
        for v in range(Y):
            gc(g, v).wait_recv()
        rows = pl.ds(g * group, group)
        if g == 0:
            for j in range(tiles):
                for copy in weight_copies(j):
                    copy.wait()

        @pl.loop(0, tiles)
        def _(j):
            cols = pl.ds(pl.multiple_of(j * TILE, TILE), TILE)
            x = rows_buf[rows, 0:width]
            gate = jnp.dot(x, gate_w[:, cols], preferred_element_type=F32)
            up = jnp.dot(x, up_w[:, cols], preferred_element_type=F32)
            hidden[:, cols] = (gate / (1.0 + jnp.exp(-gate)) * up).astype(BF16)

    def project(g):
        sends_done(g)
        rows = pl.ds(g * group, group)
        route_all = rows_buf[rows, width:width + LANES].astype(F32)
        spots = lax.broadcasted_iota(jnp.int32, (group, LANES), 1)
        column = jnp.sum(jnp.where(spots == expert, route_all, 0.0), axis=1, keepdims=True)
        for p in range(pieces):
            if g == 0:
                down_copy(p).wait()

            @pl.loop(0, part // TILE)
            def _(i):
                cols = pl.ds(pl.multiple_of(p * part + i * TILE, TILE), TILE)
                term = jnp.dot(hidden[...], down_w[:, cols], preferred_element_type=F32)
                rows_buf[rows, cols] = (column * term).astype(BF16)

            rc(g, p).start()

    spread(0)
    for g in range(1, min(planes, 3)):
        spread(g)
    pass_on(0)
    for g in range(planes):
        gate_up(g)
        if g + 1 < planes:
            pass_on(g + 1)
        if 2 < g + 3 < planes:
            spread(g + 3)
        if g >= 1:
            for p in range(pieces):
                core_sum(g - 1, p)
        project(g)
        if g >= 1:
            for p in range(pieces):
                y_sum(g - 1, p)
    last = planes - 1
    for p in range(pieces):
        core_sum(last, p)
    for p in range(pieces):
        y_sum(last, p)
    for p in range(pieces):
        for g in range(1, planes):
            rz(g, p).wait_recv()

        @pl.loop(0, part // TILE)
        def _(i):
            cols = pl.ds(pl.multiple_of(p * part + i * TILE, TILE), TILE)
            total = rows_buf[0:own, cols].astype(F32)
            for g in range(1, planes):
                total += from_z[(g - 1) * own:g * own, cols].astype(F32)
            out_ref[:, cols] = total.astype(BF16)

    for g in range(planes):
        for p in range(pieces):
            rc(g, p).wait_send()
            ry(g, p).wait_send()
            if g:
                rz(g, p).wait_send()


def local(quant_rows, block_scales, expert_ids, route_gates, gate_proj, up_proj, down_proj):
    lane_total = lax.axis_size("lane")
    planes = lane_total // Y
    span_count = lane_total // EXP_GRP
    own, width = quant_rows.shape
    units = gate_proj.shape[2]
    pieces = 4
    rows = planes * Y * CORES * own
    dma = pltpu.SemaphoreType.DMA
    vmem = pl.BlockSpec(memory_space=pltpu.VMEM)
    hbm = pl.BlockSpec(memory_space=pl.ANY)
    return pl.pallas_call(
        functools.partial(kernel, planes, pieces, span_count),
        out_shape=jax.ShapeDtypeStruct((own, width), BF16),
        in_specs=[vmem] * 4 + [hbm] * 3,
        out_specs=vmem,
        scratch_shapes=[
            pltpu.VMEM((width, units), BF16),
            pltpu.VMEM((width, units), BF16),
            pltpu.VMEM((units, width), BF16),
            pltpu.VMEM((rows, width + LANES), BF16),
            pltpu.VMEM((Y * CORES * own, units), BF16),
            pltpu.VMEM((planes * Y * own, width), BF16),
            pltpu.VMEM((planes * own, width), BF16),
            pltpu.VMEM(((planes - 1) * own, width), BF16),
            dma((units // TILE,)), dma((units // TILE,)), dma((pieces,)),
            dma((planes,)), dma((planes,)),
            dma((planes,)), dma((planes,)),
            dma((planes * Y,)), dma((planes * Y,)),
            dma((planes * pieces,)), dma((planes * pieces,)),
            dma((planes * pieces,)), dma((planes * pieces,)),
            dma((planes * pieces,)), dma((planes * pieces,)),
        ],
        compiler_params=pltpu.CompilerParams(
            collective_id=0, has_side_effects=True, vmem_limit_bytes=62 << 20
        ),
    )(quant_rows, block_scales, expert_ids, route_gates, gate_proj, up_proj, down_proj)


def solution(mesh):
    rows = P(("parts", "node", "lane"), None)
    weights = P(("node", "lane"), None, None)
    return jax.shard_map(
        local,
        mesh=mesh,
        in_specs=(rows,) * 4 + (weights,) * 3,
        out_specs=rows,
        check_vma=False,
    )
```

time: 241 us -> 135 us (0.56); the launches traced: 238 us -> 135 us
  Pallas kernels: 0 us -> 130 us
  waiting for transfers between devices: 103 us -> 0 us
  blocking collectives: 60.1 us -> 0 us
  matrix products: 51.3 us -> 0 us
  between operations: 13.4 us -> 0.01 us
  local copies, waits for them, and re-layouts: 8.99 us -> 4.54 us
    pallas_call x0 -> x1, Pallas kernels: none -> 130 us  [local(): pl.pallas_call(functools.partial(kernel, planes, pieces, span_count), out...]
    reduce_scatter x1 -> x0, waiting for transfers between devices: 91 us -> none  [local(): lax.psum_scatter(expert_work(all_quant, all_scales, column).astype(jnp.bf...]
    all_gather x2 -> x0, blocking collectives: 60.1 us -> none  [the longest x1 31.1 us: local(): lax.all_gather(block_scales, ('node', 'lane'), axis=0, tiled=True)]
    dot_general x3 -> x0, matrix products: 51.3 us -> none  [the longest x1 18.4 us: expert_terms(): up_out = jnp.dot(inputs, up_proj[0], preferred_element_type=jnp.float32)]
    all_gather x1 -> x0, waiting for transfers between devices: 11.5 us -> none  [local(): lax.all_gather(quant_rows, ('node', 'lane'), axis=0, tiled=True)]
    mul x1 -> x0, local copies, waits for them, and re-layouts: 8.88 us -> none  [dequantize(): quant_part.astype(jnp.float32)]
    unnamed x1 -> x3, local copies, waits for them, and re-layouts: 0.1 us -> 4.54 us
  transfers between devices with their start and end apart: 2 -> 0, of which waited for: 2 -> 0; matrix products, arithmetic and copies ran while one was open for 1% -> 0% of each run, Pallas kernels for 0% -> 0%
where the time goes in v1:
time: 135 us
  Pallas kernels  130 us (96%)
  local copies, waits for them, and re-layouts  4.54 us (3%)
    pallas_call x1, Pallas kernels, local(): pl.pallas_call(functools.partial(kernel, planes, pieces, span_count), out...  130 us
    unnamed x3, local copies, waits for them, and re-layouts  4.54 us

profile of v1, /device:TPU:16, one launch (start us, length us, event | category | flops | bytes accessed | tf_op | source)
XLA Modules:
  0.0 134.8 jit_solution(4284189481918733387)
XLA Ops:
  0.0 1.4 %copy.9.gates_ref = bf16[32,4]{1,0:T(8,128)(2,1)} copy(bf16[32,4]{0,1:T(4,128)(2,1)} %param.10) | data formatting | bytes 512 | tf_op args[3]
  1.4 1.4 %copy.8.ids_ref = s32[32,4]{1,0:T(8,128)} copy(s32[32,4]{0,1:T(4,128)} %param.9) | data formatting | bytes 1024 | tf_op args[2]
  2.7 130.3 %shard_map.73 = bf16[32,7168]{1,0:T(8,128)(2,1)} custom-call(bf16[32,7168]{1,0:T(8,128)(2,1)} %quant_ref.1, bf16[32,56]{1,0:T(8,128)(2,1)} %scale_ref.1, s32[32,4]{1,0:T(8,128)} %copy.8.ids_ref, bf16[32,4]{1,0:T(8,128)(2,1)} %copy.9.gates_ref, bf16[1,7168,1024]{2,1,0:T(8,128)(2,1)} %gate_hbm.1, bf16[1,7168,1024]{2,1,0:T(8,128)(2,1)} %up_hbm.1, ...), custom_call_target="tpu_custom_call" | custom-call | tf_op jit(solution)/shard_map/pallas_call | solution.py:277
  133.0 1.8 %copy.11 = bf16[32,7168]{1,0:T(8,128)(2,1)} copy(bf16[32,7168]{1,0:T(8,128)(2,1)} %shard_map.73) | data formatting | bytes 917504

commit v2 on v1

--- a/solution.py
+++ b/solution.py
@@ -103,11 +103,23 @@
             send_sem=gz_send.at[g], recv_sem=gz_recv.at[g],
             device_id=lane_z(bit), device_id_type=MESH)
 
+    last = planes - 1
+    half = own // 2
+
     def gy(g):
-        return pltpu.make_async_remote_copy(
-            src_ref=rows_buf.at[slot(g, 0, 0)], dst_ref=rows_buf.at[slot(g, 0, 1)],
+        count = half if g == last else own
+        return pltpu.make_async_remote_copy(
+            src_ref=rows_buf.at[pl.ds(g * group, count)],
+            dst_ref=rows_buf.at[pl.ds(g * group + own, count)],
             send_sem=gy_send.at[g], recv_sem=gy_recv.at[g],
             device_id=lane_y, device_id_type=MESH)
+
+    def gz_half():
+        return pltpu.make_async_remote_copy(
+            src_ref=rows_buf.at[pl.ds((last ^ 1) * group + own + half, half)],
+            dst_ref=rows_buf.at[pl.ds(last * group + own + half, half)],
+            send_sem=gz_send.at[0], recv_sem=gz_recv.at[0],
+            device_id=lane_z(1), device_id_type=MESH)
 
     def gc(g, v):
         return pltpu.make_async_remote_copy(
@@ -126,18 +138,27 @@
     def spread(g):
         if g:
             gz(g).wait_recv()
-        for child in children(g):
+        following = children(g) if g else []
+        if g & (g - 1) == 0:
+            following = ([max(2 * g, 1)] if max(2 * g, 1) < planes else []) + following
+        for child in following:
             gz(child).start()
         gy(g).start()
         gc(g, 0).start()
 
     def pass_on(g):
         gy(g).wait_recv()
+        if g == last ^ 1:
+            gz_half().start()
+        if g == last:
+            gz_half().wait_recv()
         gc(g, 1).start()
 
     def sends_done(g):
         for child in children(g):
             gz(child).wait_send()
+        if g == last ^ 1:
+            gz_half().wait_send()
         gy(g).wait_send()
         for v in range(Y):
             gc(g, v).wait_send()
@@ -220,17 +241,18 @@
                 rows_buf[rows, cols] = (column * term).astype(BF16)
 
             rc(g, p).start()
+            if g == last and p:
+                core_sum(g, p - 1)
 
     spread(0)
-    for g in range(1, min(planes, 3)):
-        spread(g)
+    spread(1)
     pass_on(0)
     for g in range(planes):
         gate_up(g)
         if g + 1 < planes:
             pass_on(g + 1)
-        if 2 < g + 3 < planes:
-            spread(g + 3)
+        if g + 2 < planes:
+            spread(g + 2)
         if g >= 1:
             for p in range(pieces):
                 core_sum(g - 1, p)
@@ -238,9 +260,7 @@
         if g >= 1:
             for p in range(pieces):
                 y_sum(g - 1, p)
-    last = planes - 1
-    for p in range(pieces):
-        core_sum(last, p)
+    core_sum(last, pieces - 1)
     for p in range(pieces):
         y_sum(last, p)
     for p in range(pieces):

time: 135 us -> 142 us (1.052)
  Pallas kernels: 130 us -> 136 us
    pallas_call x1, Pallas kernels: 130 us -> 136 us  [local(): pl.pallas_call(functools.partial(kernel, planes, pieces, span_count), out...]
where the time goes in v2:
time: 142 us; the launch traced here: 140 us
  Pallas kernels  136 us (96%)
  local copies, waits for them, and re-layouts  4.54 us (3%)
    pallas_call x1, Pallas kernels, local(): pl.pallas_call(functools.partial(kernel, planes, pieces, span_count), out...  136 us
    unnamed x3, local copies, waits for them, and re-layouts  4.54 us

profile of v2, /device:TPU:16, one launch (start us, length us, event | category | flops | bytes accessed | tf_op | source)
XLA Modules:
  0.0 140.5 jit_solution(18252179427225341063)
XLA Ops:
  0.0 1.4 copy.9.gates_ref
  1.4 1.4 copy.8.ids_ref
  2.7 136.0 %shard_map.73 = bf16[32,7168]{1,0:T(8,128)(2,1)} custom-call(bf16[32,7168]{1,0:T(8,128)(2,1)} %quant_ref.1, bf16[32,56]{1,0:T(8,128)(2,1)} %scale_ref.1, s32[32,4]{1,0:T(8,128)} %copy.8.ids_ref, bf16[32,4]{1,0:T(8,128)(2,1)} %copy.9.gates_ref, bf16[1,7168,1024]{2,1,0:T(8,128)(2,1)} %gate_hbm.1, bf16[1,7168,1024]{2,1,0:T(8,128)(2,1)} %up_hbm.1, ...), custom_call_target="tpu_custom_call" | custom-call | tf_op jit(solution)/shard_map/pallas_call | solution.py:297
  138.7 1.8 %copy.11 = bf16[32,7168]{1,0:T(8,128)(2,1)} copy(bf16[32,7168]{1,0:T(8,128)(2,1)} %shard_map.73) | data formatting | bytes 917504

commit v3 on v1

--- a/solution.py
+++ b/solution.py
@@ -54,6 +54,8 @@
     lane_y = {"lane": z * Y + (1 - y)}
     other_core = {"node": 1 - node}
 
+    order = list(range(1, planes)) + [0]
+
     def weight_copies(j):
         cols = pl.ds(j * TILE, TILE)
         return (
@@ -190,7 +192,7 @@
         for v in range(Y):
             gc(g, v).wait_recv()
         rows = pl.ds(g * group, group)
-        if g == 0:
+        if g == order[0]:
             for j in range(tiles):
                 for copy in weight_copies(j):
                     copy.wait()
@@ -210,7 +212,7 @@
         spots = lax.broadcasted_iota(jnp.int32, (group, LANES), 1)
         column = jnp.sum(jnp.where(spots == expert, route_all, 0.0), axis=1, keepdims=True)
         for p in range(pieces):
-            if g == 0:
+            if g == order[0]:
                 down_copy(p).wait()
 
             @pl.loop(0, part // TILE)
@@ -221,28 +223,24 @@
 
             rc(g, p).start()
 
-    spread(0)
-    for g in range(1, min(planes, 3)):
+    for g in range(min(planes, 3)):
         spread(g)
-    pass_on(0)
-    for g in range(planes):
+    for g in range(2):
+        pass_on(g)
+    for i, g in enumerate(order):
         gate_up(g)
-        if g + 1 < planes:
-            pass_on(g + 1)
-        if 2 < g + 3 < planes:
-            spread(g + 3)
-        if g >= 1:
-            for p in range(pieces):
-                core_sum(g - 1, p)
+        if 3 + i < planes:
+            spread(3 + i)
+        if 2 + i < planes:
+            pass_on(2 + i)
+        for back, step in ((1, core_sum), (2, y_sum)):
+            if i >= back:
+                for p in range(pieces):
+                    step(order[i - back], p)
         project(g)
-        if g >= 1:
-            for p in range(pieces):
-                y_sum(g - 1, p)
-    last = planes - 1
-    for p in range(pieces):
-        core_sum(last, p)
-    for p in range(pieces):
-        y_sum(last, p)
+    for step, g in ((core_sum, order[-1]), (y_sum, order[-2]), (y_sum, order[-1])):
+        for p in range(pieces):
+            step(g, p)
     for p in range(pieces):
         for g in range(1, planes):
             rz(g, p).wait_recv()

time: 135 us -> 123 us (0.911)
  Pallas kernels: 130 us -> 118 us
    pallas_call x1, Pallas kernels: 130 us -> 118 us  [local(): pl.pallas_call(functools.partial(kernel, planes, pieces, span_count), out...]
where the time goes in v3:
time: 123 us
  Pallas kernels  118 us (96%)
  local copies, waits for them, and re-layouts  4.54 us (4%)
    pallas_call x1, Pallas kernels, local(): pl.pallas_call(functools.partial(kernel, planes, pieces, span_count), out...  118 us
    unnamed x3, local copies, waits for them, and re-layouts  4.54 us

profile of v3, /device:TPU:16, one launch (start us, length us, event | category | flops | bytes accessed | tf_op | source)
XLA Modules:
  0.0 122.8 jit_solution(11684412607204519232)
XLA Ops:
  0.0 1.4 %copy.9.gates_ref = bf16[32,4]{1,0:T(8,128)(2,1)} copy(bf16[32,4]{0,1:T(4,128)(2,1)} %param.10) | data formatting | bytes 512 | tf_op args[3]
  1.4 1.4 %copy.8.ids_ref = s32[32,4]{1,0:T(8,128)} copy(s32[32,4]{0,1:T(4,128)} %param.9) | data formatting | bytes 1024 | tf_op args[2]
  2.7 118.3 %shard_map.73 = bf16[32,7168]{1,0:T(8,128)(2,1)} custom-call(bf16[32,7168]{1,0:T(8,128)(2,1)} %quant_ref.1, bf16[32,56]{1,0:T(8,128)(2,1)} %scale_ref.1, s32[32,4]{1,0:T(8,128)} %copy.8.ids_ref, bf16[32,4]{1,0:T(8,128)(2,1)} %copy.9.gates_ref, bf16[1,7168,1024]{2,1,0:T(8,128)(2,1)} %gate_hbm.1, bf16[1,7168,1024]{2,1,0:T(8,128)(2,1)} %up_hbm.1, ...), custom_call_target="tpu_custom_call" | custom-call | tf_op jit(solution)/shard_map/pallas_call | solution.py:275
  121.0 1.8 %copy.11 = bf16[32,7168]{1,0:T(8,128)(2,1)} copy(bf16[32,7168]{1,0:T(8,128)(2,1)} %shard_map.73) | data formatting | bytes 917504
